TPU v7x, 32 devices: a whole 2x2x4 slice. The times are simulated.
32 devices in a mesh: tp: 2 (over core), grp: 8 (over z, y), rep: 2 (over x).
Axes of the slice: x: 2, y: 2, z: 4, core: 2. Of those that a mesh axis runs over, the one named last changes fastest.
Arguments:
- tokens: bfloat16 [2048, 4096], P(('rep', 'tp', 'grp')), parts along dimension 0, may hold values from -6 to 6
- qkv_weight: bfloat16 [4096, 5120], P(None, ('tp', 'grp')), may hold values from -0.09375 to 0.09375
- qkv_bias: bfloat16 [5120], replicated, may hold values from -3 to 3
- cache: bfloat16 [128, 1024, 1024], P(('rep', 'tp', 'grp')), parts along dimension 0, may hold values from -80 to 80
- lengths: int32 [128], P('rep'), parts along dimension 0, may hold values from 128 to 1024, as said below
- slot_stream: int32 [128], P('rep'), parts along dimension 0, may hold values from 0 to 63, each once
Outputs:
- attended: bfloat16 [2048, 4096], P(('rep', 'tp', 'grp')), parts along dimension 0
There are 2 independent parts, one for each index of `rep`. A program takes and returns all parts, laid end to end along the dimension named above; an argument that names none is the same for every part. Nothing has to cross between parts.
Inputs may be any that keep to these rules, and one draw needn't show every extreme that they name: `lengths`: cache length of each stream; some stream has exactly 1024 and some exactly 128. `slot_stream`: each stream appears in exactly one slot.
All inputs are finite; a program needn't handle non-finite values.
Results may differ from a plain program's by a relative error of at most 0.004.
The roundings to bfloat16 on the way count: a program that leaves them out, or rounds other values in their place, can miss the bound.
Values may be sent and summed in bfloat16 or wider, within the bound.
A program may use at most 128 MiB of HBM per device.

v0:
```python
import jax
import jax.numpy as jnp
from jax import lax
from jax.sharding import PartitionSpec as P

HD = 128
HQ = 32
KVH = 4
STRETCH = 16
CAP = 1024
GROUP = 8


ROPE_THETA = 1000000.0


def rotate(vectors, positions):
    half_width = vectors.shape[-1] // 2
    frequency = ROPE_THETA ** (
        -(jnp.arange(half_width, dtype=jnp.float32) * 2.0) / vectors.shape[-1]
    )
    angles = positions.astype(jnp.float32)[:, None] * frequency[None, :]
    cosine = jnp.cos(angles)[:, None, :]
    sine_part = jnp.sin(angles)[:, None, :]
    front_half = vectors[..., :half_width]
    back_half = vectors[..., half_width:]
    return jnp.concatenate(
        [front_half * cosine - back_half * sine_part, back_half * cosine + front_half * sine_part],
        axis=-1,
    )


def attend(token_block, slot_cache, length):
    query_width = HQ * HD
    kv_width = KVH * HD
    positions = length + jnp.arange(STRETCH, dtype=jnp.int32)
    queries = rotate(
        token_block[:, :query_width].astype(jnp.float32).reshape(STRETCH, HQ, HD), positions
    ).astype(jnp.bfloat16)
    new_keys = rotate(
        token_block[:, query_width : query_width + kv_width]
        .astype(jnp.float32)
        .reshape(STRETCH, KVH, HD),
        positions,
    ).astype(jnp.bfloat16)
    new_values = token_block[:, query_width + kv_width :].reshape(STRETCH, KVH, HD)
    grouped = (
        queries.reshape(STRETCH, KVH, GROUP, HD)
        .transpose(1, 0, 2, 3)
        .reshape(KVH, STRETCH * GROUP, HD)
    )
    score_scale = HD ** (-0.5)
    query_token = jnp.arange(STRETCH * GROUP, dtype=jnp.int32) // GROUP
    scores = (
        jnp.einsum("krd,jkd->krj", grouped, new_keys, preferred_element_type=jnp.float32)
        * score_scale
    )
    causal = jnp.arange(STRETCH, dtype=jnp.int32)[None, :] <= query_token[:, None]
    scores = jnp.where(causal[None], scores, -jnp.inf)
    row_max = jnp.max(scores, axis=-1)
    exponent = jnp.exp(scores - row_max[..., None])
    row_total = jnp.sum(exponent, axis=-1)
    running = jnp.einsum(
        "krj,jkd->krd",
        exponent.astype(jnp.bfloat16),
        new_values,
        preferred_element_type=jnp.float32,
    )
    key_span = min(CAP, 256)
    key_part = slot_cache[:, :kv_width]
    value_part = slot_cache[:, kv_width:]

    def visit(block_index, running_state):
        old_max, old_total, old_sum = running_state
        offset = block_index * key_span
        key_block = lax.dynamic_slice_in_dim(key_part, offset, key_span, 0).reshape(
            key_span, KVH, HD
        )
        value_block = lax.dynamic_slice_in_dim(value_part, offset, key_span, 0).reshape(
            key_span, KVH, HD
        )
        block_scores = (
            jnp.einsum("krd,jkd->krj", grouped, key_block, preferred_element_type=jnp.float32)
            * score_scale
        )
        in_cache = offset + jnp.arange(key_span, dtype=jnp.int32) < length
        block_scores = jnp.where(in_cache[None, None, :], block_scores, -jnp.inf)
        new_max = jnp.maximum(old_max, jnp.max(block_scores, axis=-1))
        rescale = jnp.exp(old_max - new_max)
        block_exp = jnp.exp(block_scores - new_max[..., None])
        new_total = old_total * rescale + jnp.sum(block_exp, axis=-1)
        new_sum = old_sum * rescale[..., None] + jnp.einsum(
            "krj,jkd->krd",
            block_exp.astype(jnp.bfloat16),
            value_block,
            preferred_element_type=jnp.float32,
        )
        return (new_max, new_total, new_sum)

    block_count = CAP // key_span
    row_max, row_total, running = lax.fori_loop(
        0, block_count, visit, (row_max, row_total, running)
    )
    result = running / row_total[..., None]
    return (
        result.reshape(KVH, STRETCH, GROUP, HD)
        .transpose(1, 0, 2, 3)
        .reshape(STRETCH, HQ * HD)
        .astype(jnp.bfloat16)
    )


def on_device(tokens, qkv_weight, qkv_bias, cache, lengths, slot_stream):
    my_index = lax.axis_index(("tp", "grp"))
    grp_index = lax.axis_index("grp")
    tp_count = lax.axis_size("tp")
    grp_count = lax.axis_size("grp")
    per_device = cache.shape[0]
    local_rows = per_device * STRETCH
    shard_cols = qkv_weight.shape[1]
    weight_cols = lax.all_gather(qkv_weight, "tp", axis=1, tiled=True)
    bias_table = qkv_bias.reshape(tp_count, grp_count, shard_cols)
    bias_cols = (
        lax.dynamic_index_in_dim(bias_table, grp_index, 1, keepdims=False)
        .reshape(-1)
        .astype(jnp.float32)
    )
    partial_cols = jnp.dot(
        lax.all_gather(tokens, "grp", axis=0, tiled=True),
        weight_cols,
        preferred_element_type=jnp.float32,
    )
    rounded_cols = (partial_cols + bias_cols[None, :]).astype(jnp.bfloat16)
    received = lax.all_to_all(rounded_cols, "grp", split_axis=0, concat_axis=1, tiled=True)
    projected_qkv = (
        received.reshape(local_rows, grp_count, tp_count, shard_cols)
        .transpose(0, 2, 1, 3)
        .reshape(local_rows, -1)
    )
    my_slots = my_index * per_device + jnp.arange(per_device, dtype=jnp.int32)
    my_lengths = jnp.take(lengths, jnp.take(slot_stream, my_slots))
    attended = jnp.concatenate(
        [
            attend(
                projected_qkv[slot_index * STRETCH : (slot_index + 1) * STRETCH],
                cache[slot_index],
                my_lengths[slot_index],
            )
            for slot_index in range(per_device)
        ],
        axis=0,
    )
    return attended


def solution(mesh):
    in_specs = (
        P(("rep", "tp", "grp"), None),
        P(None, ("tp", "grp")),
        P(),
        P(("rep", "tp", "grp"), None, None),
        P("rep"),
        P("rep"),
    )
    out_specs = P(("rep", "tp", "grp"), None)
    return jax.shard_map(
        on_device, mesh=mesh, in_specs=in_specs, out_specs=out_specs, check_vma=False
    )
```

profile of v0, /device:TPU:0, one launch (start us, length us, event | category | flops | bytes accessed | tf_op | source)
XLA Modules:
  0.0 189.3 jit_solution(472580984637509546)
XLA Ops:
  6.5 0.7 all-gather.5.cloned.1.call-update
  7.3 0.7 all-gather.3.cloned.1.call-update
  8.2 6.0 %fusion.89 = (bf16[1,1024,1024]{2,1,0:T(8,128)(2,1)}, bf16[1,1024,1024]{2,1,0:T(8,128)(2,1)}, bf16[1,1024,1024]{2,1,0:T(8,128)(2,1)}, bf16[1,1024,1024]{2,1,0:T(8,128)(2,1)}) fusion(bf16[4,1024,1024]{2,1,0:T(8,128)(2,1)} %param.19), kind=kLoop, calls=%fused_computation.195 | loop fusion | bytes 16777216 | tf_op jit(solution)/shard_map/slice | solution.py:146
  14.2 2.9 %copy.148 = bf16[1,1024,1024]{1,2,0:T(8,128)(2,1)S(1)} copy(bf16[1,1024,1024]{2,1,0:T(8,128)(2,1)} %get-tuple-element.662) | data formatting | bytes 4194304
  17.2 0.6 gather_fusion
  17.8 0.6 gather_fusion.1
  18.5 0.7 fusion.99
  20.4 0.7 add_convert_fusion.8
  21.1 1.5 fusion.90
  22.6 4.3 %all-gather.5.cloned.1.call-done = bf16[4096,640]{0,1:T(8,128)(2,1)} async-done(((bf16[4096,320]{0,1:T(8,128)(2,1)}), bf16[4096,640]{0,1:T(8,128)(2,1)}) %all-gather.5.cloned.1.call-update) | async-done | bytes 5242896 | tf_op jit(solution)/shard_map/all_gather | solution.py:121
  26.9 76.7 %all-gather.3.cloned.1.call-done = bf16[512,4096]{1,0:T(8,128)(2,1)} async-done(((bf16[64,4096]{1,0:T(8,128)(2,1)}), bf16[512,4096]{1,0:T(8,128)(2,1)}) %all-gather.3.cloned.1.call-update) | async-done | bytes 4194320 | tf_op jit(solution)/shard_map/all_gather | solution.py:129
  103.6 8.1 %fusion.24 = bf16[512,640]{1,0:T(8,128)(2,1)} fusion(bf16[512,4096]{1,0:T(8,128)(2,1)} %all-gather.3.cloned.1.call-done, bf16[4096,640]{0,1:T(8,128)(2,1)} %all-gather.5.cloned.1.call-done, f32[640]{0:T(1024)S(1)} %reshape.502), kind=kOutput, calls=%fused_computation.55 | convolution fusion | flops 2685009920 | bytes 10095104 | tf_op jit(solution)/shard_map/dot_general | solution.py:128
  111.7 4.4 %all-to-all-start = ((bf16[8,64,640]{2,1,0:T(8,128)(2,1)}), bf16[8,64,640]{2,1,0:T(8,128)(2,1)}, u32[]{:S(2)}, u32[]{:S(2)}) async-start(bf16[8,64,640]{2,1,0:T(8,128)(2,1)} %bitcast.12), calls=%async_computation | async-start | bytes 1310720 | tf_op jit(solution)/shard_map/all_to_all | solution.py:134
  116.7 4.1 %copy.151 = bf16[1,1024,1024]{1,2,0:T(8,128)(2,1)} copy(bf16[1,1024,1024]{2,1,0:T(8,128)(2,1)} %get-tuple-element.664) | data formatting | bytes 4194304
  120.8 2.6 %copy.154 = bf16[1,1024,1024]{1,2,0:T(8,128)(2,1)} copy(bf16[1,1024,1024]{2,1,0:T(8,128)(2,1)S(1)} %copy-done.3) | data formatting | bytes 4194304
  123.3 2.9 %copy.157 = bf16[1,1024,1024]{1,2,0:T(8,128)(2,1)S(1)} copy(bf16[1,1024,1024]{2,1,0:T(8,128)(2,1)} %get-tuple-element.665) | data formatting | bytes 4194304
  126.4 3.2 %fusion.91 = (bf16[1024,512]{0,1:T(8,128)(2,1)}, bf16[1024,512]{0,1:T(8,128)(2,1)}) fusion(bf16[1024,1024]{0,1:T(8,128)(2,1)} %bitcast.224), kind=kLoop, calls=%fused_computation.197 | loop fusion | bytes 4194304 | tf_op jit(solution)/shard_map/slice | solution.py:71
  129.6 1.5 fusion.92
  131.1 1.1 fusion.93
  132.3 2.4 %reshape.541 = bf16[64,8,2,320]{3,2,0,1:T(2,128)(2,1)S(1)} reshape(bf16[64,8,640]{2,0,1:T(8,128)(2,1)} %bitcast.13) | data formatting | bytes 1310720 | tf_op jit(solution)/shard_map/reshape | solution.py:136
  138.1 9.8 %while.68 = (s32[]{:T(128)}, f32[4,128]{1,0:T(4,128)S(1)}, f32[4,128]{1,0:T(4,128)S(1)}, f32[4,128,128]{2,1,0:T(8,128)S(1)}, s32[]{:T(128)}, /*index=5*/bf16[102...) while((s32[]{:T(128)}, f32[4,128]{1,0:T(4,128)S(1)}, ...), condition=%wide.region_5.7_spmd, body=%wide.region_2.6_spmd.sunk | while | flops 68158976 | bytes 3834543 | solution.py:101
  138.1 1.1 constant_dynamic-slice_fusion.12
  140.6 1.1 constant_dynamic-slice_fusion.12
  143.1 1.1 constant_dynamic-slice_fusion.12
  145.5 1.1 constant_dynamic-slice_fusion.12
  148.9 10.0 %while.69 = (s32[]{:T(128)}, f32[4,128]{1,0:T(4,128)S(1)}, f32[4,128]{1,0:T(4,128)S(1)}, f32[4,128,128]{2,1,0:T(8,128)S(1)}, s32[]{:T(128)}, /*index=5*/bf16[102...) while((s32[]{:T(128)}, f32[4,128]{1,0:T(4,128)S(1)}, ...), condition=%wide.region_11.13_spmd, body=%wide.region_8.12_spmd.sunk | while | flops 68158976 | bytes 3834543 | solution.py:101
  148.9 1.1 constant_dynamic-slice_fusion.13
  150.0 0.6 add_compare_fusion.9
  151.4 1.1 constant_dynamic-slice_fusion.13
  152.5 0.6 add_compare_fusion.9
  153.9 1.1 constant_dynamic-slice_fusion.13
  155.0 0.6 add_compare_fusion.9
  156.4 1.1 constant_dynamic-slice_fusion.13
  160.4 10.0 %while.70 = (s32[]{:T(128)}, f32[4,128]{1,0:T(4,128)S(1)}, f32[4,128]{1,0:T(4,128)S(1)}, f32[4,128,128]{2,1,0:T(8,128)S(1)}, s32[]{:T(128)}, /*index=5*/bf16[102...) while((s32[]{:T(128)}, f32[4,128]{1,0:T(4,128)S(1)}, ...), condition=%wide.region_17.19_spmd, body=%wide.region_14.18_spmd.sunk | while | flops 68158976 | bytes 3834543 | solution.py:101
  160.5 1.1 constant_dynamic-slice_fusion.14
  163.0 1.1 constant_dynamic-slice_fusion.14
  165.4 1.1 constant_dynamic-slice_fusion.14
  167.9 1.1 constant_dynamic-slice_fusion.14
  171.3 10.0 %while.71 = (s32[]{:T(128)}, f32[4,128]{1,0:T(4,128)S(1)}, f32[4,128]{1,0:T(4,128)S(1)}, f32[4,128,128]{2,1,0:T(8,128)S(1)}, s32[]{:T(128)}, /*index=5*/bf16[102...) while((s32[]{:T(128)}, f32[4,128]{1,0:T(4,128)S(1)}, ...), condition=%wide.region_23.25_spmd, body=%wide.region_20.24_spmd.sunk | while | flops 68158976 | bytes 3834543 | solution.py:101
  171.4 1.0 constant_dynamic-slice_fusion.15
  172.4 0.7 add_compare_fusion.11
  173.9 1.0 constant_dynamic-slice_fusion.15
  174.9 0.7 add_compare_fusion.11
  176.4 1.0 constant_dynamic-slice_fusion.15
  177.4 0.7 add_compare_fusion.11
  178.9 1.0 constant_dynamic-slice_fusion.15
  179.9 0.7 add_compare_fusion.11
  181.6 0.8 pad_maximum_fusion
  (195 shorter events, 26.4 us)
Async XLA Ops:
  6.5 10.6 %copy-start = (s32[64]{0:T(128)S(1)}, s32[64]{0:T(128)}, u32[]{:S(2)}) copy-start(s32[64]{0:T(128)} %param.21) | copy-start | bytes 772
  6.5 1.5 copy-start.4
  6.5 20.3 %all-gather.5.cloned.1.call-start = ((), (), s32[]{:S(2)}) async-start(), calls=%async_computation.2 | async-start | bytes 7864320 | tf_op jit(solution)/shard_map/all_gather | solution.py:121
  7.3 96.3 %all-gather.3.cloned.1.call-start = ((), (), s32[]{:S(2)}) async-start(), calls=%async_computation.1 | async-start | bytes 4718592 | tf_op jit(solution)/shard_map/all_gather | solution.py:129
  14.2 3.6 %copy-start.1 = (s32[64]{0:T(128)S(1)}, s32[64]{0:T(128)}, u32[]{:S(2)}) copy-start(s32[64]{0:T(128)} %param.20) | copy-start | bytes 772
  111.7 20.6 %all-to-all-start = ((bf16[8,64,640]{2,1,0:T(8,128)(2,1)}), bf16[8,64,640]{2,1,0:T(8,128)(2,1)}, u32[]{:S(2)}, u32[]{:S(2)}) async-start(bf16[8,64,640]{2,1,0:T(8,128)(2,1)} %bitcast.12), calls=%async_computation | async-start | bytes 1310720 | tf_op jit(solution)/shard_map/all_to_all | solution.py:134
  116.7 4.1 %copy-start.3 = (bf16[1,1024,1024]{2,1,0:T(8,128)(2,1)S(1)}, bf16[1,1024,1024]{2,1,0:T(8,128)(2,1)}, u32[]{:S(2)}) copy-start(bf16[1,1024,1024]{2,1,0:T(8,128)(2,1)} %get-tuple-element.663) | copy-start | bytes 6291460
  126.4 3.2 %copy-start.2 = (bf16[1,1024,1024]{1,2,0:T(8,128)(2,1)S(1)}, bf16[1,1024,1024]{1,2,0:T(8,128)(2,1)}, u32[]{:S(2)}) copy-start(bf16[1,1024,1024]{1,2,0:T(8,128)(2,1)} %copy.154) | copy-start | bytes 6291460
Sparse Core Ops, SparseCore 0:
  8.9 17.9 all-gather.4
  29.0 74.5 all-gather.2
where the time goes:
time: 190 us; the launch traced here: 189 us
  waiting for transfers between devices  82.4 us (43%)
  local copies, waits for them, and re-layouts  50 us (26%)
  matrix products  20.3 us (11%)
  other arithmetic  17.3 us (9%)
  between operations  14 us (7%)
  starting transfers between devices  4.42 us (2%)
    all_gather x1, waiting for transfers between devices, on_device(): lax.all_gather(tokens, 'grp', axis=0, tiled=True)  76.7 us
    dynamic_slice x16, local copies, waits for them, and re-layouts, visit(): lax.dynamic_slice_in_dim(value_part, offset, key_span, 0)  16.9 us
    unnamed x22, local copies, waits for them, and re-layouts  12.8 us
    lt x16, other arithmetic, visit(): in_cache = offset + jnp.arange(key_span, dtype=jnp.int32) < length  10 us
    dot_general x1, matrix products, on_device(): jnp.dot(lax.all_gather(tokens, 'grp', axis=0, tiled=True), weight_cols, p...  8.09 us
    slice x4, local copies, waits for them, and re-layouts, attend(): value_part = slot_cache[:, kv_width:]  7.32 us
    slice x1, local copies, waits for them, and re-layouts, on_device(): cache[slot_index]  6.02 us
    dot_general x16, matrix products, visit(): jnp.einsum('krj,jkd->krd', block_exp.astype(jnp.bfloat16), value_block, p...  5.41 us
  transfers between devices with their start and end apart: 3, of which 3 were waited for; matrix products, arithmetic and copies ran while one was open for 16% of the time, Pallas kernels for 0%

commit v1 on v0

--- a/solution.py
+++ b/solution.py
@@ -1,6 +1,10 @@
+import functools
+
 import jax
 import jax.numpy as jnp
 from jax import lax
+from jax.experimental import pallas as pl
+from jax.experimental.pallas import tpu as pltpu
 from jax.sharding import PartitionSpec as P
 
 HD = 128
@@ -153,7 +157,344 @@
     return attended
 
 
+MESH = pl.DeviceIdType.MESH
+LOG2E = 1.4426950408889634
+
+
+def fused_kernel(
+    n,
+    groups,
+    cols,
+    tokens_ref,
+    weight_ref,
+    bias_ref,
+    cache_ref,
+    lengths_ref,
+    streams_ref,
+    freq_ref,
+    out_ref,
+    tok,
+    weights,
+    slots,
+    acc,
+    outgoing,
+    incoming,
+    cos_table,
+    sin_table,
+    tok_local,
+    tok_send,
+    tok_recv,
+    part_send,
+    part_recv,
+    weight_sems,
+    cache_sems,
+):
+    tp = lax.axis_index("tp")
+    me = lax.axis_index("grp")
+    chain = groups // 2
+    depth = me // 2
+    side = me % 2
+    across = depth * 2 + 1 - side
+    wide = acc.shape[1]
+    first_slot = (tp * groups + me) * n
+
+    def local_tokens(c):
+        return pltpu.make_async_copy(
+            tokens_ref.at[pl.ds(pl.multiple_of(c * STRETCH, STRETCH), STRETCH)],
+            tok.at[c, me],
+            tok_local.at[c],
+        )
+
+    def cache_copy(c):
+        return pltpu.make_async_copy(cache_ref.at[c], slots.at[c], cache_sems.at[c])
+
+    def tok_copy(c, block, direction, target):
+        return pltpu.make_async_remote_copy(
+            src_ref=tok.at[c, block],
+            dst_ref=tok.at[c, block],
+            send_sem=tok_send.at[c, block, direction],
+            recv_sem=tok_recv.at[c, block],
+            device_id={"grp": target},
+            device_id_type=MESH,
+        )
+
+    def part_copy(c, peer):
+        return pltpu.make_async_remote_copy(
+            src_ref=outgoing.at[c, peer],
+            dst_ref=incoming.at[c, me],
+            send_sem=part_send.at[c, peer],
+            recv_sem=part_recv.at[c, me],
+            device_id={"grp": peer},
+            device_id_type=MESH,
+        )
+
+    def part_arrival(c, peer):
+        return pltpu.make_async_remote_copy(
+            src_ref=outgoing.at[c, peer],
+            dst_ref=incoming.at[c, peer],
+            send_sem=part_send.at[c, peer],
+            recv_sem=part_recv.at[c, peer],
+            device_id={"grp": peer},
+            device_id_type=MESH,
+        )
+
+    weight_own = pltpu.make_async_copy(weight_ref, weights.at[tp], weight_sems.at[0])
+    weight_swap = pltpu.make_async_remote_copy(
+        src_ref=weight_ref,
+        dst_ref=weights.at[tp],
+        send_sem=weight_sems.at[1],
+        recv_sem=weight_sems.at[2],
+        device_id={"tp": 1 - tp},
+        device_id_type=MESH,
+    )
+
+    for c in range(n):
+        local_tokens(c).start()
+
+    barrier = pltpu.get_barrier_semaphore()
+    pl.semaphore_signal(barrier, inc=1, device_id={"tp": 1 - tp}, device_id_type=MESH)
+    for d in range(1, groups):
+        pl.semaphore_signal(
+            barrier, inc=1, device_id={"grp": lax.rem(me + d, groups)}, device_id_type=MESH
+        )
+    pl.semaphore_wait(barrier, groups)
+
+    def send_own(c):
+        local_tokens(c).wait()
+        tok_copy(c, me, 2, across).start()
+
+        @pl.when(depth + 1 < chain)
+        def _():
+            tok_copy(c, me, 0, me + 2).start()
+
+        @pl.when(depth >= 1)
+        def _():
+            tok_copy(c, me, 1, me - 2).start()
+
+    def forward(c, s):
+        @pl.when(depth >= s)
+        def _():
+            block = me - 2 * s
+            tok_copy(c, block, 2, across).wait_recv()
+            tok_copy(c, block, 2, across).start()
+
+            @pl.when(depth + 1 < chain)
+            def _():
+                tok_copy(c, block, 0, me + 2).start()
+
+        @pl.when(depth + s < chain)
+        def _():
+            block = me + 2 * s
+            tok_copy(c, block, 2, across).wait_recv()
+            tok_copy(c, block, 2, across).start()
+
+            @pl.when(depth >= 1)
+            def _():
+                tok_copy(c, block, 1, me - 2).start()
+
+    def finish_sends(c):
+        for level in range(chain):
+            block = level * 2 + side
+            tok_copy(c, block, 2, across).wait_send()
+
+            @pl.when((level <= depth) & (depth + 1 < chain))
+            def _():
+                tok_copy(c, block, 0, me + 2).wait_send()
+
+            @pl.when((level >= depth) & (depth >= 1))
+            def _():
+                tok_copy(c, block, 1, me - 2).wait_send()
+
+        for d in range(1, groups):
+            part_copy(c, lax.rem(me + d, groups)).wait_send()
+
+    def project(c):
+        for level in range(chain):
+            tok_copy(c, level * 2 + 1 - side, 2, across).wait_recv()
+        rows = tok[c].reshape(groups * STRETCH, tok.shape[3])
+        for t in range(2):
+            acc[:, :cols] = (
+                jnp.dot(rows, weights[t], preferred_element_type=jnp.float32)
+                + bias_ref[t * groups + me]
+            )
+            moved = pltpu.roll(acc[...], (wide - cols) * side, 1)
+            outgoing[c, :, t] = moved.astype(jnp.bfloat16).reshape(groups, STRETCH, wide)
+        for d in range(1, groups):
+            part_copy(c, lax.rem(me + d, groups)).start()
+        incoming[c, me] = outgoing[c, me]
+
+    lane = lax.broadcasted_iota(jnp.int32, (STRETCH, HD), 1)
+    rows_all = STRETCH * GROUP
+    pair_heads = 2 * cols // HD
+    half = groups // 2 * pair_heads
+
+    def attention(c):
+        for d in range(1, groups):
+            part_arrival(c, lax.rem(me + d, groups)).wait_recv()
+        cache_copy(c).wait()
+        length = lengths_ref[streams_ref[first_slot + c]]
+        cosine = cos_table[c]
+        sine = sin_table[c]
+        key_index = lax.broadcasted_iota(jnp.int32, (1, CAP), 1)
+        in_cache = key_index < length
+        new_index = lax.broadcasted_iota(jnp.int32, (rows_all, STRETCH), 1)
+        new_token = lax.broadcasted_iota(jnp.int32, (rows_all, STRETCH), 0) % STRETCH
+        causal = new_index <= new_token
+        factor = HD ** (-0.5) * LOG2E
+        middle = pair_heads // 2
+
+        def head(i):
+            t, rest = divmod(i, half)
+            pair, k = divmod(rest, pair_heads)
+            if k < middle:
+                return incoming[c, 2 * pair, t, :, k * HD : (k + 1) * HD]
+            right = incoming[c, 2 * pair + 1, t, :, (k - middle) * HD : (k - middle + 1) * HD]
+            if k > middle:
+                return right
+            left = incoming[c, 2 * pair, t, :, k * HD : (k + 1) * HD]
+            return jnp.where(
+                lane < HD // 2, left.astype(jnp.float32), right.astype(jnp.float32)
+            ).astype(jnp.bfloat16)
+
+        def rotated(i):
+            u = head(i).astype(jnp.float32)
+            return (u * cosine + pltpu.roll(u, HD // 2, 1) * sine).astype(jnp.bfloat16)
+
+        nt = (((1,), (1,)), ((), ()))
+        for k in range(KVH):
+            queries = jnp.concatenate([rotated(k * GROUP + g) for g in range(GROUP)], axis=0)
+            new_keys = rotated(HQ + k)
+            new_values = head(HQ + KVH + k)
+            keys = slots[c, :, k * HD : (k + 1) * HD]
+            values = slots[c, :, (KVH + k) * HD : (KVH + k + 1) * HD]
+            scores = lax.dot_general(queries, keys, nt, preferred_element_type=jnp.float32)
+            scores = jnp.where(in_cache, scores, -jnp.inf)
+            new_scores = lax.dot_general(queries, new_keys, nt, preferred_element_type=jnp.float32)
+            new_scores = jnp.where(causal, new_scores, -jnp.inf)
+            top = jnp.maximum(
+                jnp.max(scores, axis=-1, keepdims=True), jnp.max(new_scores, axis=-1, keepdims=True)
+            )
+            probs = jnp.exp2((scores - top) * factor)
+            new_probs = jnp.exp2((new_scores - top) * factor)
+            total = jnp.sum(probs, axis=-1, keepdims=True) + jnp.sum(
+                new_probs, axis=-1, keepdims=True
+            )
+            summed = jnp.dot(
+                probs.astype(jnp.bfloat16), values, preferred_element_type=jnp.float32
+            ) + jnp.dot(
+                new_probs.astype(jnp.bfloat16), new_values, preferred_element_type=jnp.float32
+            )
+            result = (summed / total).astype(jnp.bfloat16)
+            for g in range(GROUP):
+                h = k * GROUP + g
+                out_ref[
+                    pl.ds(pl.multiple_of(c * STRETCH, STRETCH), STRETCH), h * HD : (h + 1) * HD
+                ] = result[g * STRETCH : (g + 1) * STRETCH]
+
+    for c in range(min(2, n)):
+        send_own(c)
+    weight_own.start()
+    weight_swap.start()
+    for c in range(n):
+        cache_copy(c).start()
+
+    acc[...] = jnp.zeros_like(acc)
+    sign = jnp.where(lane < HD // 2, -1.0, 1.0)
+    token = lax.broadcasted_iota(jnp.int32, (STRETCH, HD), 0)
+    for c in range(n):
+        length = lengths_ref[streams_ref[first_slot + c]]
+        angles = (length + token).astype(jnp.float32) * freq_ref[...]
+        cos_table[c] = jnp.cos(angles)
+        sin_table[c] = jnp.sin(angles) * sign
+
+    @pl.loop(0, n + 2)
+    def _(i):
+        @pl.when(i < n)
+        def _():
+            forward(i, 1)
+
+        @pl.when(i == 1)
+        def _():
+            weight_own.wait()
+            weight_swap.wait()
+
+        @pl.when((i >= 1) & (i < n + 1))
+        def _():
+            project(i - 1)
+
+        @pl.when(i < n)
+        def _():
+            for s in range(2, chain):
+                forward(i, s)
+
+        @pl.when(i + 2 < n)
+        def _():
+            send_own(i + 2)
+
+        @pl.when(i >= 2)
+        def _():
+            attention(i - 2)
+
+    @pl.loop(0, n)
+    def _(c):
+        finish_sends(c)
+
+
+def fused(tokens, qkv_weight, qkv_bias, cache, lengths, slot_stream):
+    groups = lax.axis_size("grp")
+    n = cache.shape[0]
+    width, cols = qkv_weight.shape
+    wide = cols + HD // 2
+    bias = qkv_bias.astype(jnp.float32).reshape(2 * groups, 1, cols)
+    frequency = ROPE_THETA ** (-(jnp.arange(HD // 2, dtype=jnp.float32) * 2.0) / HD)
+    frequency = jnp.concatenate([frequency, frequency])[None, :]
+    anywhere = pl.BlockSpec(memory_space=pl.ANY)
+    vmem = pl.BlockSpec(memory_space=pltpu.VMEM)
+    smem = pl.BlockSpec(memory_space=pltpu.SMEM)
+    dma = pltpu.SemaphoreType.DMA
+    rows = groups * STRETCH
+    attention_ops = 4 * n * KVH * STRETCH * GROUP * CAP * HD
+    return pl.pallas_call(
+        functools.partial(fused_kernel, n, groups, cols),
+        out_shape=jax.ShapeDtypeStruct((n * STRETCH, HQ * HD), jnp.bfloat16),
+        in_specs=[anywhere, anywhere, vmem, anywhere, smem, smem, vmem],
+        out_specs=vmem,
+        scratch_shapes=[
+            pltpu.VMEM((n, groups, STRETCH, width), jnp.bfloat16),
+            pltpu.VMEM((2, width, cols), jnp.bfloat16),
+            pltpu.VMEM(cache.shape, jnp.bfloat16),
+            pltpu.VMEM((rows, wide), jnp.float32),
+            pltpu.VMEM((n, groups, 2, STRETCH, wide), jnp.bfloat16),
+            pltpu.VMEM((n, groups, 2, STRETCH, wide), jnp.bfloat16),
+            pltpu.VMEM((n, STRETCH, HD), jnp.float32),
+            pltpu.VMEM((n, STRETCH, HD), jnp.float32),
+            dma((n,)),
+            dma((n, groups, 3)),
+            dma((n, groups)),
+            dma((n, groups)),
+            dma((n, groups)),
+            dma((3,)),
+            dma((n,)),
+        ],
+        compiler_params=pltpu.CompilerParams(
+            collective_id=0, has_side_effects=True, vmem_limit_bytes=56 * 2**20
+        ),
+        cost_estimate=pl.CostEstimate(
+            flops=4 * n * rows * width * cols + attention_ops,
+            bytes_accessed=2 * (cache.size + 2 * qkv_weight.size),
+            transcendentals=n * KVH * STRETCH * GROUP * CAP,
+        ),
+    )(tokens, qkv_weight, bias, cache, lengths, slot_stream, frequency)
+
+
 def solution(mesh):
+    def program(tokens, qkv_weight, qkv_bias, cache, lengths, slot_stream):
+        cols = qkv_weight.shape[1]
+        groups = lax.axis_size("grp")
+        fits = lax.axis_size("tp") == 2 and groups % 2 == 0 and cols % HD == HD // 2
+        body = fused if fits else on_device
+        return body(tokens, qkv_weight, qkv_bias, cache, lengths, slot_stream)
+
     in_specs = (
         P(("rep", "tp", "grp"), None),
         P(None, ("tp", "grp")),
@@ -164,5 +505,5 @@
     )
     out_specs = P(("rep", "tp", "grp"), None)
     return jax.shard_map(
-        on_device, mesh=mesh, in_specs=in_specs, out_specs=out_specs, check_vma=False
-    )
+        program, mesh=mesh, in_specs=in_specs, out_specs=out_specs, check_vma=False
+    )

time: 190 us -> 79.7 us (0.42)
  waiting for transfers between devices: 82.4 us -> 0 us
  Pallas kernels: 0 us -> 71 us
  local copies, waits for them, and re-layouts: 50 us -> 7.81 us
  matrix products: 20.3 us -> 0 us
  other arithmetic: 17.3 us -> 0.6 us
  between operations: 14 us -> 0.01 us
  starting transfers between devices: 4.42 us -> 0 us
    all_gather x2 -> x0, waiting for transfers between devices: 81 us -> none  [the longest x1 76.7 us: on_device(): lax.all_gather(tokens, 'grp', axis=0, tiled=True)]
    pallas_call x0 -> x1, Pallas kernels: none -> 71 us  [fused(): pl.pallas_call(functools.partial(fused_kernel, n, groups, cols), out_shap...]
    dot_general x41 -> x0, matrix products: 20.3 us -> none  [the longest x1 8.09 us: on_device(): jnp.dot(lax.all_gather(tokens, 'grp', axis=0, tiled=True), weight_cols, p...]
    dynamic_slice x16 -> x0, local copies, waits for them, and re-layouts: 16.9 us -> none  [visit(): lax.dynamic_slice_in_dim(value_part, offset, key_span, 0)]
    slice x19 -> x0, local copies, waits for them, and re-layouts: 15.7 us -> none  [the longest x4 7.32 us: attend(): value_part = slot_cache[:, kv_width:]]
    lt x16 -> x0, other arithmetic: 10 us -> none  [visit(): in_cache = offset + jnp.arange(key_span, dtype=jnp.int32) < length]
    unnamed x22 -> x2, local copies, waits for them, and re-layouts: 12.8 us -> 6.41 us
    all_to_all x1 -> x0, starting transfers between devices: 4.38 us -> none  [on_device(): lax.all_to_all(rounded_cols, 'grp', split_axis=0, concat_axis=1, tiled=True)]
  transfers between devices with their start and end apart: 3 -> 0, of which waited for: 3 -> 0; matrix products, arithmetic and copies ran while one was open for 16% -> 0% of each run, Pallas kernels for 0% -> 0%
where the time goes in v1:
time: 79.7 us; the launch traced here: 79.4 us
  Pallas kernels  71 us (89%)
  local copies, waits for them, and re-layouts  7.81 us (10%)
    pallas_call x1, Pallas kernels, fused(): pl.pallas_call(functools.partial(fused_kernel, n, groups, cols), out_shap...  71 us
    unnamed x2, local copies, waits for them, and re-layouts  6.41 us

profile of v1, /device:TPU:0, one launch (start us, length us, event | category | flops | bytes accessed | tf_op | source)
XLA Modules:
  0.0 79.4 jit_solution(1828536882692857238)
XLA Ops:
  0.0 0.6 maximum_bitcast_fusion.freq_ref
  0.6 1.4 %reshape.8.bias_ref = f32[16,1,320]{2,1,0:T(1,128)} reshape(bf16[5120]{0:T(1024)(128)(2,1)} %param.8) | data formatting | bytes 30720 | tf_op jit(solution)/shard_map/reshape | solution.py:448
  2.0 4.5 %copy.7.weight_ref = bf16[4096,320]{1,0:T(8,128)(2,1)} copy(bf16[4096,320]{0,1:T(8,128)(2,1)} %param.7) | data formatting | bytes 5242880 | tf_op args[1]
  6.5 71.0 %shard_map.64 = bf16[64,4096]{1,0:T(8,128)(2,1)} custom-call(bf16[64,4096]{1,0:T(8,128)(2,1)} %tokens_ref.1, bf16[4096,320]{1,0:T(8,128)(2,1)} %copy.7.weight_ref, f32[16,1,320]{2,1,0:T(1,128)} %reshape.8.bias_ref, bf16[4,1024,1024]{2,1,0:T(8,128)(2,1)} %cache_ref.1, s32[64]{0:T(128)} %lengths_ref.1, s32[64]{0:T(128)} %streams_ref.1, ...), custom_call_target="tpu_custom_call" | custom-call | flops 3758096384 | bytes 13631488 | tf_op jit(solution)/shard_map/pallas_call | solution.py:457
  77.5 1.9 %copy.9 = bf16[64,4096]{1,0:T(8,128)(2,1)} copy(bf16[64,4096]{1,0:T(8,128)(2,1)} %shard_map.64) | data formatting | bytes 1048576
  (1 shorter events, 0.0 us)

commit v2 on v1

--- a/solution.py
+++ b/solution.py
@@ -2,6 +2,7 @@
 
 import jax
 import jax.numpy as jnp
+import numpy as np
 from jax import lax
 from jax.experimental import pallas as pl
 from jax.experimental.pallas import tpu as pltpu
@@ -176,7 +177,7 @@
     tok,
     weights,
     slots,
-    acc,
+    bias,
     outgoing,
     incoming,
     cos_table,
@@ -195,7 +196,7 @@
     depth = me // 2
     side = me % 2
     across = depth * 2 + 1 - side
-    wide = acc.shape[1]
+    main = cols - HD // 2
     first_slot = (tp * groups + me) * n
 
     def local_tokens(c):
@@ -238,15 +239,29 @@
             device_id_type=MESH,
         )
 
-    weight_own = pltpu.make_async_copy(weight_ref, weights.at[tp], weight_sems.at[0])
-    weight_swap = pltpu.make_async_remote_copy(
-        src_ref=weight_ref,
-        dst_ref=weights.at[tp],
-        send_sem=weight_sems.at[1],
-        recv_sem=weight_sems.at[2],
-        device_id={"tp": 1 - tp},
-        device_id_type=MESH,
-    )
+    pieces = (
+        (HD // 2 * side, main, (main + HD) * tp),
+        (main * (1 - side), HD // 2, main + HD // 2 * ((tp + side) % 2)),
+    )
+
+    def weight_own(p):
+        start, size, at = pieces[p]
+        return pltpu.make_async_copy(
+            weight_ref.at[pl.ds(pl.multiple_of(start, HD // 2), size)],
+            weights.at[pl.ds(pl.multiple_of(at, HD // 2), size)],
+            weight_sems.at[p, 0],
+        )
+
+    def weight_swap(p):
+        start, size, at = pieces[p]
+        return pltpu.make_async_remote_copy(
+            src_ref=weight_ref.at[pl.ds(pl.multiple_of(start, HD // 2), size)],
+            dst_ref=weights.at[pl.ds(pl.multiple_of(at, HD // 2), size)],
+            send_sem=weight_sems.at[p, 1],
+            recv_sem=weight_sems.at[p, 2],
+            device_id={"tp": 1 - tp},
+            device_id_type=MESH,
+        )
 
     for c in range(n):
         local_tokens(c).start()
@@ -292,6 +307,8 @@
             def _():
                 tok_copy(c, block, 1, me - 2).start()
 
+    nt = (((1,), (1,)), ((), ()))
+
     def finish_sends(c):
         for level in range(chain):
             block = level * 2 + side
@@ -312,13 +329,9 @@
         for level in range(chain):
             tok_copy(c, level * 2 + 1 - side, 2, across).wait_recv()
         rows = tok[c].reshape(groups * STRETCH, tok.shape[3])
-        for t in range(2):
-            acc[:, :cols] = (
-                jnp.dot(rows, weights[t], preferred_element_type=jnp.float32)
-                + bias_ref[t * groups + me]
-            )
-            moved = pltpu.roll(acc[...], (wide - cols) * side, 1)
-            outgoing[c, :, t] = moved.astype(jnp.bfloat16).reshape(groups, STRETCH, wide)
+        product = lax.dot_general(rows, weights[...], nt, preferred_element_type=jnp.float32)
+        product = (product + bias[...]).astype(jnp.bfloat16)
+        outgoing[c] = product.reshape(groups, STRETCH, 2 * cols)
         for d in range(1, groups):
             part_copy(c, lax.rem(me + d, groups)).start()
         incoming[c, me] = outgoing[c, me]
@@ -327,6 +340,7 @@
     rows_all = STRETCH * GROUP
     pair_heads = 2 * cols // HD
     half = groups // 2 * pair_heads
+    middle = pair_heads // 2
 
     def attention(c):
         for d in range(1, groups):
@@ -341,26 +355,26 @@
         new_token = lax.broadcasted_iota(jnp.int32, (rows_all, STRETCH), 0) % STRETCH
         causal = new_index <= new_token
         factor = HD ** (-0.5) * LOG2E
-        middle = pair_heads // 2
 
         def head(i):
             t, rest = divmod(i, half)
             pair, k = divmod(rest, pair_heads)
-            if k < middle:
-                return incoming[c, 2 * pair, t, :, k * HD : (k + 1) * HD]
-            right = incoming[c, 2 * pair + 1, t, :, (k - middle) * HD : (k - middle + 1) * HD]
-            if k > middle:
-                return right
-            left = incoming[c, 2 * pair, t, :, k * HD : (k + 1) * HD]
-            return jnp.where(
-                lane < HD // 2, left.astype(jnp.float32), right.astype(jnp.float32)
-            ).astype(jnp.bfloat16)
+            if k != middle:
+                block, at = (2 * pair, k) if k < middle else (2 * pair + 1, k - middle - 1)
+                at = at * HD + t * (main + HD)
+                return incoming[c, block, :, at : at + HD]
+            left = incoming[c, 2 * pair, :, main : main + HD].astype(jnp.float32)
+            right = incoming[c, 2 * pair + 1, :, main : main + HD].astype(jnp.float32)
+            if t == 0:
+                joined = jnp.where(lane < HD // 2, left, right)
+            else:
+                joined = pltpu.roll(jnp.where(lane < HD // 2, right, left), HD // 2, 1)
+            return joined.astype(jnp.bfloat16)
 
         def rotated(i):
             u = head(i).astype(jnp.float32)
             return (u * cosine + pltpu.roll(u, HD // 2, 1) * sine).astype(jnp.bfloat16)
 
-        nt = (((1,), (1,)), ((), ()))
         for k in range(KVH):
             queries = jnp.concatenate([rotated(k * GROUP + g) for g in range(GROUP)], axis=0)
             new_keys = rotated(HQ + k)
@@ -393,12 +407,25 @@
 
     for c in range(min(2, n)):
         send_own(c)
-    weight_own.start()
-    weight_swap.start()
+    for p in range(2):
+        weight_own(p).start()
+        weight_swap(p).start()
     for c in range(n):
         cache_copy(c).start()
 
-    acc[...] = jnp.zeros_like(acc)
+    first_head = depth * pair_heads
+
+    def bias_heads(start, count):
+        at = pl.multiple_of(start * HD, HD)
+        return bias_ref[:, pl.ds(at, count * HD)].astype(jnp.float32)
+
+    for t in range(2):
+        whole = bias_heads(t * half + first_head + (middle + 1) * side, middle)
+        bias[:, t * (main + HD) : t * (main + HD) + main] = whole
+    joint = [bias_heads(t * half + first_head + middle, 1) for t in range(2)]
+    front = lax.broadcasted_iota(jnp.int32, (1, HD), 1) // (HD // 2) == side
+    bias[:, main : main + HD] = jnp.where(front, joint[0], pltpu.roll(joint[1], HD // 2, 1))
+
     sign = jnp.where(lane < HD // 2, -1.0, 1.0)
     token = lax.broadcasted_iota(jnp.int32, (STRETCH, HD), 0)
     for c in range(n):
@@ -415,8 +442,9 @@
 
         @pl.when(i == 1)
         def _():
-            weight_own.wait()
-            weight_swap.wait()
+            for p in range(2):
+                weight_own(p).wait()
+                weight_swap(p).wait()
 
         @pl.when((i >= 1) & (i < n + 1))
         def _():
@@ -444,10 +472,8 @@
     groups = lax.axis_size("grp")
     n = cache.shape[0]
     width, cols = qkv_weight.shape
-    wide = cols + HD // 2
-    bias = qkv_bias.astype(jnp.float32).reshape(2 * groups, 1, cols)
-    frequency = ROPE_THETA ** (-(jnp.arange(HD // 2, dtype=jnp.float32) * 2.0) / HD)
-    frequency = jnp.concatenate([frequency, frequency])[None, :]
+    frequency = ROPE_THETA ** (-(np.arange(HD // 2) * 2.0) / HD)
+    frequency = np.concatenate([frequency, frequency])[None, :].astype(np.float32)
     anywhere = pl.BlockSpec(memory_space=pl.ANY)
     vmem = pl.BlockSpec(memory_space=pltpu.VMEM)
     smem = pl.BlockSpec(memory_space=pltpu.SMEM)
@@ -461,11 +487,11 @@
         out_specs=vmem,
         scratch_shapes=[
             pltpu.VMEM((n, groups, STRETCH, width), jnp.bfloat16),
-            pltpu.VMEM((2, width, cols), jnp.bfloat16),
+            pltpu.VMEM((2 * cols, width), jnp.bfloat16),
             pltpu.VMEM(cache.shape, jnp.bfloat16),
-            pltpu.VMEM((rows, wide), jnp.float32),
-            pltpu.VMEM((n, groups, 2, STRETCH, wide), jnp.bfloat16),
-            pltpu.VMEM((n, groups, 2, STRETCH, wide), jnp.bfloat16),
+            pltpu.VMEM((1, 2 * cols), jnp.float32),
+            pltpu.VMEM((n, groups, STRETCH, 2 * cols), jnp.bfloat16),
+            pltpu.VMEM((n, groups, STRETCH, 2 * cols), jnp.bfloat16),
             pltpu.VMEM((n, STRETCH, HD), jnp.float32),
             pltpu.VMEM((n, STRETCH, HD), jnp.float32),
             dma((n,)),
@@ -473,7 +499,7 @@
             dma((n, groups)),
             dma((n, groups)),
             dma((n, groups)),
-            dma((3,)),
+            dma((2, 3)),
             dma((n,)),
         ],
         compiler_params=pltpu.CompilerParams(
@@ -484,7 +510,7 @@
             bytes_accessed=2 * (cache.size + 2 * qkv_weight.size),
             transcendentals=n * KVH * STRETCH * GROUP * CAP,
         ),
-    )(tokens, qkv_weight, bias, cache, lengths, slot_stream, frequency)
+    )(tokens, qkv_weight.T, qkv_bias[None, :], cache, lengths, slot_stream, jnp.asarray(frequency))
 
 
 def solution(mesh):

time: 79.7 us -> 73.3 us (0.920)
  local copies, waits for them, and re-layouts: 7.81 us -> 3.19 us
  Pallas kernels: 71 us -> 69.9 us
    unnamed x2 -> x1, local copies, waits for them, and re-layouts: 6.41 us -> 1.87 us
    reshape x1 -> x0, local copies, waits for them, and re-layouts: 1.4 us -> none  [fused(): bias = qkv_bias.astype(jnp.float32).reshape(2 * groups, 1, cols)]
    broadcast_in_dim x0 -> x1, local copies, waits for them, and re-layouts: none -> 1.32 us  [fused(): qkv_bias[None, :]]
    pallas_call x1, Pallas kernels: 71 us -> 69.9 us  [fused(): pl.pallas_call(functools.partial(fused_kernel, n, groups, cols), out_shap...]
where the time goes in v2:
time: 73.3 us; the launch traced here: 73.1 us
  Pallas kernels  69.9 us (95%)
  local copies, waits for them, and re-layouts  3.19 us (4%)
    pallas_call x1, Pallas kernels, fused(): pl.pallas_call(functools.partial(fused_kernel, n, groups, cols), out_shap...  69.9 us
    unnamed x1, local copies, waits for them, and re-layouts  1.87 us

profile of v2, /device:TPU:0, one launch (start us, length us, event | category | flops | bytes accessed | tf_op | source)
XLA Modules:
  0.0 73.1 jit_solution(11825386309282431219)
XLA Ops:
  0.0 1.3 %broadcast_in_dim.3.bias_ref = bf16[1,5120]{1,0:T(2,128)(2,1)} reshape(bf16[5120]{0:T(1024)(128)(2,1)} %param.9) | data formatting | bytes 20480 | tf_op jit(solution)/shard_map/broadcast_in_dim | solution.py:513
  1.3 69.9 %shard_map.73 = bf16[64,4096]{1,0:T(8,128)(2,1)} custom-call(bf16[64,4096]{1,0:T(8,128)(2,1)} %tokens_ref.1, bf16[320,4096]{1,0:T(8,128)(2,1)} %bitcast.1, bf16[1,5120]{1,0:T(2,128)(2,1)} %broadcast_in_dim.3.bias_ref, bf16[4,1024,1024]{2,1,0:T(8,128)(2,1)} %cache_ref.1, s32[64]{0:T(128)} %lengths_ref.1, s32[64]{0:T(128)} %streams_ref.1, ...), custom_call_target="tpu_custom_call" | custom-call | flops 3758096384 | bytes 13631488 | tf_op jit(solution)/shard_map/pallas_call | solution.py:483
  71.2 1.9 %copy.9 = bf16[64,4096]{1,0:T(8,128)(2,1)} copy(bf16[64,4096]{1,0:T(8,128)(2,1)} %shard_map.73) | data formatting | bytes 1048576

commit v3 on v2

--- a/solution.py
+++ b/solution.py
@@ -189,6 +189,7 @@
     part_recv,
     weight_sems,
     cache_sems,
+    relay_sems,
 ):
     tp = lax.axis_index("tp")
     me = lax.axis_index("grp")
@@ -196,6 +197,9 @@
     depth = me // 2
     side = me % 2
     across = depth * 2 + 1 - side
+    paired = depth + 1 - 2 * (depth % 2)
+    width = tok.shape[3]
+    split = width * 11 // 32 // HD * HD
     main = cols - HD // 2
     first_slot = (tp * groups + me) * n
 
@@ -216,6 +220,28 @@
             send_sem=tok_send.at[c, block, direction],
             recv_sem=tok_recv.at[c, block],
             device_id={"grp": target},
+            device_id_type=MESH,
+        )
+
+    def rest_copy(c, block):
+        part = tok.at[c, block, :, pl.ds(split, width - split)]
+        return pltpu.make_async_remote_copy(
+            src_ref=part,
+            dst_ref=part,
+            send_sem=tok_send.at[c, block, 2],
+            recv_sem=tok_recv.at[c, block],
+            device_id={"grp": across},
+            device_id_type=MESH,
+        )
+
+    def relay_copy(c, level):
+        part = tok.at[c, level * 2 + 1 - side, :, pl.ds(0, split)]
+        return pltpu.make_async_remote_copy(
+            src_ref=part,
+            dst_ref=part,
+            send_sem=relay_sems.at[c, 0],
+            recv_sem=relay_sems.at[c, 1],
+            device_id={"grp": paired * 2 + side},
             device_id_type=MESH,
         )
 
@@ -286,12 +312,25 @@
         def _():
             tok_copy(c, me, 1, me - 2).start()
 
+    def send_across(c, block, shared):
+        @pl.when(shared)
+        def _():
+            rest_copy(c, block).start()
+
+        @pl.when(jnp.logical_not(shared))
+        def _():
+            tok_copy(c, block, 2, across).start()
+
+    def relay(c):
+        tok_copy(c, across, 2, across).wait_recv()
+        relay_copy(c, depth).start()
+
     def forward(c, s):
         @pl.when(depth >= s)
         def _():
             block = me - 2 * s
             tok_copy(c, block, 2, across).wait_recv()
-            tok_copy(c, block, 2, across).start()
+            send_across(c, block, (s == 1) & (depth % 2 == 1))
 
             @pl.when(depth + 1 < chain)
             def _():
@@ -301,7 +340,7 @@
         def _():
             block = me + 2 * s
             tok_copy(c, block, 2, across).wait_recv()
-            tok_copy(c, block, 2, across).start()
+            send_across(c, block, (s == 1) & (depth % 2 == 0))
 
             @pl.when(depth >= 1)
             def _():
@@ -312,7 +351,14 @@
     def finish_sends(c):
         for level in range(chain):
             block = level * 2 + side
-            tok_copy(c, block, 2, across).wait_send()
+
+            @pl.when(level == paired)
+            def _():
+                rest_copy(c, block).wait_send()
+
+            @pl.when(level != paired)
+            def _():
+                tok_copy(c, block, 2, across).wait_send()
 
             @pl.when((level <= depth) & (depth + 1 < chain))
             def _():
@@ -322,12 +368,23 @@
             def _():
                 tok_copy(c, block, 1, me - 2).wait_send()
 
+        relay_copy(c, depth).wait_send()
         for d in range(1, groups):
             part_copy(c, lax.rem(me + d, groups)).wait_send()
 
     def project(c):
         for level in range(chain):
-            tok_copy(c, level * 2 + 1 - side, 2, across).wait_recv()
+            block = level * 2 + 1 - side
+
+            @pl.when((level != paired) & (level != depth))
+            def _():
+                tok_copy(c, block, 2, across).wait_recv()
+
+            @pl.when(level == paired)
+            def _():
+                rest_copy(c, block).wait_recv()
+                relay_copy(c, level).wait_recv()
+
         rows = tok[c].reshape(groups * STRETCH, tok.shape[3])
         product = lax.dot_general(rows, weights[...], nt, preferred_element_type=jnp.float32)
         product = (product + bias[...]).astype(jnp.bfloat16)
@@ -439,6 +496,7 @@
         @pl.when(i < n)
         def _():
             forward(i, 1)
+            relay(i)
 
         @pl.when(i == 1)
         def _():
@@ -501,6 +559,7 @@
             dma((n, groups)),
             dma((2, 3)),
             dma((n,)),
+            dma((n, 2)),
         ],
         compiler_params=pltpu.CompilerParams(
             collective_id=0, has_side_effects=True, vmem_limit_bytes=56 * 2**20
@@ -517,7 +576,7 @@
     def program(tokens, qkv_weight, qkv_bias, cache, lengths, slot_stream):
         cols = qkv_weight.shape[1]
         groups = lax.axis_size("grp")
-        fits = lax.axis_size("tp") == 2 and groups % 2 == 0 and cols % HD == HD // 2
+        fits = lax.axis_size("tp") == 2 and groups % 4 == 0 and cols % HD == HD // 2
         body = fused if fits else on_device
         return body(tokens, qkv_weight, qkv_bias, cache, lengths, slot_stream)
 

time: 73.3 us -> 73.2 us (level)
  no operation moved by 1% of the time
where the time goes in v3:
time: 73.2 us; the launch traced here: 72.9 us
  Pallas kernels  69.7 us (95%)
  local copies, waits for them, and re-layouts  3.19 us (4%)
    pallas_call x1, Pallas kernels, fused(): pl.pallas_call(functools.partial(fused_kernel, n, groups, cols), out_shap...  69.7 us
    unnamed x1, local copies, waits for them, and re-layouts  1.87 us

profile of v3, /device:TPU:0, one launch (start us, length us, event | category | flops | bytes accessed | tf_op | source)
XLA Modules:
  0.0 72.9 jit_solution(1847618805387811365)
XLA Ops:
  0.0 1.3 %broadcast_in_dim.3.bias_ref = bf16[1,5120]{1,0:T(2,128)(2,1)} reshape(bf16[5120]{0:T(1024)(128)(2,1)} %param.9) | data formatting | bytes 20480 | tf_op jit(solution)/shard_map/broadcast_in_dim | solution.py:572
  1.3 69.7 %shard_map.73 = bf16[64,4096]{1,0:T(8,128)(2,1)} custom-call(bf16[64,4096]{1,0:T(8,128)(2,1)} %tokens_ref.1, bf16[320,4096]{1,0:T(8,128)(2,1)} %bitcast.1, bf16[1,5120]{1,0:T(2,128)(2,1)} %broadcast_in_dim.3.bias_ref, bf16[4,1024,1024]{2,1,0:T(8,128)(2,1)} %cache_ref.1, s32[64]{0:T(128)} %lengths_ref.1, s32[64]{0:T(128)} %streams_ref.1, ...), custom_call_target="tpu_custom_call" | custom-call | flops 3758096384 | bytes 13631488 | tf_op jit(solution)/shard_map/pallas_call | solution.py:541
  71.0 1.9 %copy.9 = bf16[64,4096]{1,0:T(8,128)(2,1)} copy(bf16[64,4096]{1,0:T(8,128)(2,1)} %shard_map.73) | data formatting | bytes 1048576

commit v4 on v3

--- a/solution.py
+++ b/solution.py
@@ -190,6 +190,9 @@
     weight_sems,
     cache_sems,
     relay_sems,
+    bias_all,
+    done,
+    out_sems,
 ):
     tp = lax.axis_index("tp")
     me = lax.axis_index("grp")
@@ -212,6 +215,13 @@
 
     def cache_copy(c):
         return pltpu.make_async_copy(cache_ref.at[c], slots.at[c], cache_sems.at[c])
+
+    def out_copy(c):
+        return pltpu.make_async_copy(
+            done.at[c],
+            out_ref.at[pl.ds(pl.multiple_of(c * STRETCH, STRETCH), STRETCH)],
+            out_sems.at[c],
+        )
 
     def tok_copy(c, block, direction, target):
         return pltpu.make_async_remote_copy(
@@ -458,23 +468,25 @@
             result = (summed / total).astype(jnp.bfloat16)
             for g in range(GROUP):
                 h = k * GROUP + g
-                out_ref[
-                    pl.ds(pl.multiple_of(c * STRETCH, STRETCH), STRETCH), h * HD : (h + 1) * HD
-                ] = result[g * STRETCH : (g + 1) * STRETCH]
-
-    for c in range(min(2, n)):
-        send_own(c)
+                done[c, :, h * HD : (h + 1) * HD] = result[g * STRETCH : (g + 1) * STRETCH]
+        out_copy(c).start()
+
+    send_own(0)
     for p in range(2):
         weight_own(p).start()
         weight_swap(p).start()
     for c in range(n):
         cache_copy(c).start()
 
+    for start in range(0, bias_ref.shape[0], 2 * HD):
+        piece = bias_ref[start : start + 2 * HD].astype(jnp.float32)
+        bias_all[:, start : start + 2 * HD] = piece.reshape(1, 2 * HD)
+
     first_head = depth * pair_heads
 
     def bias_heads(start, count):
         at = pl.multiple_of(start * HD, HD)
-        return bias_ref[:, pl.ds(at, count * HD)].astype(jnp.float32)
+        return bias_all[:, pl.ds(at, count * HD)]
 
     for t in range(2):
         whole = bias_heads(t * half + first_head + (middle + 1) * side, middle)
@@ -491,12 +503,25 @@
         cos_table[c] = jnp.cos(angles)
         sin_table[c] = jnp.sin(angles) * sign
 
-    @pl.loop(0, n + 2)
+    @pl.loop(0, n + 3)
     def _(i):
         @pl.when(i < n)
         def _():
             forward(i, 1)
+
+        @pl.when(i + 1 < n)
+        def _():
+            send_own(i + 1)
+
+        @pl.when(((i >= 2) & (i < n)) | ((i > n) & (i >= 3)))
+        def _():
+            attention(jnp.where(i < n, i - 2, i - 3))
+
+        @pl.when(i < n)
+        def _():
             relay(i)
+            for s in range(2, chain - 1):
+                forward(i, s)
 
         @pl.when(i == 1)
         def _():
@@ -510,20 +535,12 @@
 
         @pl.when(i < n)
         def _():
-            for s in range(2, chain):
-                forward(i, s)
-
-        @pl.when(i + 2 < n)
-        def _():
-            send_own(i + 2)
-
-        @pl.when(i >= 2)
-        def _():
-            attention(i - 2)
+            forward(i, chain - 1)
 
     @pl.loop(0, n)
     def _(c):
         finish_sends(c)
+        out_copy(c).wait()
 
 
 def fused(tokens, qkv_weight, qkv_bias, cache, lengths, slot_stream):
@@ -542,7 +559,7 @@
         functools.partial(fused_kernel, n, groups, cols),
         out_shape=jax.ShapeDtypeStruct((n * STRETCH, HQ * HD), jnp.bfloat16),
         in_specs=[anywhere, anywhere, vmem, anywhere, smem, smem, vmem],
-        out_specs=vmem,
+        out_specs=anywhere,
         scratch_shapes=[
             pltpu.VMEM((n, groups, STRETCH, width), jnp.bfloat16),
             pltpu.VMEM((2 * cols, width), jnp.bfloat16),
@@ -560,6 +577,9 @@
             dma((2, 3)),
             dma((n,)),
             dma((n, 2)),
+            pltpu.VMEM((1, qkv_bias.shape[0]), jnp.float32),
+            pltpu.VMEM((n, STRETCH, HQ * HD), jnp.bfloat16),
+            dma((n,)),
         ],
         compiler_params=pltpu.CompilerParams(
             collective_id=0, has_side_effects=True, vmem_limit_bytes=56 * 2**20
@@ -569,7 +589,7 @@
             bytes_accessed=2 * (cache.size + 2 * qkv_weight.size),
             transcendentals=n * KVH * STRETCH * GROUP * CAP,
         ),
-    )(tokens, qkv_weight.T, qkv_bias[None, :], cache, lengths, slot_stream, jnp.asarray(frequency))
+    )(tokens, qkv_weight.T, qkv_bias, cache, lengths, slot_stream, jnp.asarray(frequency))
 
 
 def solution(mesh):

time: 73.2 us -> 70.5 us (0.963)
  local copies, waits for them, and re-layouts: 3.19 us -> 1.87 us
  Pallas kernels: 69.7 us -> 68.4 us
    broadcast_in_dim x1 -> x0, local copies, waits for them, and re-layouts: 1.32 us -> none  [fused(): qkv_bias[None, :]]
    pallas_call x1, Pallas kernels: 69.7 us -> 68.4 us  [fused(): pl.pallas_call(functools.partial(fused_kernel, n, groups, cols), out_shap...]
where the time goes in v4:
time: 70.5 us; the launch traced here: 70.3 us
  Pallas kernels  68.4 us (97%)
  local copies, waits for them, and re-layouts  1.87 us (3%)
    pallas_call x1, Pallas kernels, fused(): pl.pallas_call(functools.partial(fused_kernel, n, groups, cols), out_shap...  68.4 us
    unnamed x1, local copies, waits for them, and re-layouts  1.87 us

profile of v4, /device:TPU:0, one launch (start us, length us, event | category | flops | bytes accessed | tf_op | source)
XLA Modules:
  0.0 70.3 jit_solution(2742511585720826271)
XLA Ops:
  0.0 68.4 %shard_map.73 = bf16[64,4096]{1,0:T(8,128)(2,1)} custom-call(bf16[64,4096]{1,0:T(8,128)(2,1)} %tokens_ref.1, bf16[320,4096]{1,0:T(8,128)(2,1)} %bitcast.1, bf16[5120]{0:T(1024)(128)(2,1)} %bias_ref.1, bf16[4,1024,1024]{2,1,0:T(8,128)(2,1)} %cache_ref.1, s32[64]{0:T(128)} %lengths_ref.1, s32[64]{0:T(128)} %streams_ref.1, f32[1,128]{1,0:T(1,128)} %constant.2.clone.freq_ref), custom_call_target="tpu_custom_call" | custom-call | flops 3758096384 | bytes 13631488 | tf_op jit(solution)/shard_map/pallas_call | solution.py:558
  68.4 1.9 %copy.9 = bf16[64,4096]{1,0:T(8,128)(2,1)} copy(bf16[64,4096]{1,0:T(8,128)(2,1)} %shard_map.73) | data formatting | bytes 1048576

commit v5 on v4

--- a/solution.py
+++ b/solution.py
@@ -191,8 +191,7 @@
     cache_sems,
     relay_sems,
     bias_all,
-    done,
-    out_sems,
+    partner_in,
 ):
     tp = lax.axis_index("tp")
     me = lax.axis_index("grp")
@@ -216,13 +215,6 @@
     def cache_copy(c):
         return pltpu.make_async_copy(cache_ref.at[c], slots.at[c], cache_sems.at[c])
 
-    def out_copy(c):
-        return pltpu.make_async_copy(
-            done.at[c],
-            out_ref.at[pl.ds(pl.multiple_of(c * STRETCH, STRETCH), STRETCH)],
-            out_sems.at[c],
-        )
-
     def tok_copy(c, block, direction, target):
         return pltpu.make_async_remote_copy(
             src_ref=tok.at[c, block],
@@ -302,13 +294,26 @@
     for c in range(n):
         local_tokens(c).start()
 
+    for p in range(2):
+        weight_own(p).start()
+    for c in range(n):
+        cache_copy(c).start()
+
     barrier = pltpu.get_barrier_semaphore()
-    pl.semaphore_signal(barrier, inc=1, device_id={"tp": 1 - tp}, device_id_type=MESH)
+
+    @pl.when(tp == 0)
+    def _():
+        pl.semaphore_signal(barrier, inc=1, device_id={"tp": 1 - tp}, device_id_type=MESH)
+
     for d in range(1, groups):
         pl.semaphore_signal(
             barrier, inc=1, device_id={"grp": lax.rem(me + d, groups)}, device_id_type=MESH
         )
-    pl.semaphore_wait(barrier, groups)
+    pl.semaphore_wait(barrier, groups - 1 + tp)
+
+    @pl.when(tp == 1)
+    def _():
+        pl.semaphore_signal(partner_in, inc=1, device_id={"tp": 1 - tp}, device_id_type=MESH)
 
     def send_own(c):
         local_tokens(c).wait()
@@ -468,15 +473,16 @@
             result = (summed / total).astype(jnp.bfloat16)
             for g in range(GROUP):
                 h = k * GROUP + g
-                done[c, :, h * HD : (h + 1) * HD] = result[g * STRETCH : (g + 1) * STRETCH]
-        out_copy(c).start()
+                out_ref[
+                    pl.ds(pl.multiple_of(c * STRETCH, STRETCH), STRETCH), h * HD : (h + 1) * HD
+                ] = result[g * STRETCH : (g + 1) * STRETCH]
 
     send_own(0)
-    for p in range(2):
-        weight_own(p).start()
-        weight_swap(p).start()
-    for c in range(n):
-        cache_copy(c).start()
+
+    @pl.when(tp == 1)
+    def _():
+        for p in range(2):
+            weight_swap(p).start()
 
     for start in range(0, bias_ref.shape[0], 2 * HD):
         piece = bias_ref[start : start + 2 * HD].astype(jnp.float32)
@@ -513,6 +519,12 @@
         def _():
             send_own(i + 1)
 
+        @pl.when((i == 0) & (tp == 0))
+        def _():
+            pl.semaphore_wait(partner_in, 1)
+            for p in range(2):
+                weight_swap(p).start()
+
         @pl.when(((i >= 2) & (i < n)) | ((i > n) & (i >= 3)))
         def _():
             attention(jnp.where(i < n, i - 2, i - 3))
@@ -540,7 +552,6 @@
     @pl.loop(0, n)
     def _(c):
         finish_sends(c)
-        out_copy(c).wait()
 
 
 def fused(tokens, qkv_weight, qkv_bias, cache, lengths, slot_stream):
@@ -557,9 +568,9 @@
     attention_ops = 4 * n * KVH * STRETCH * GROUP * CAP * HD
     return pl.pallas_call(
         functools.partial(fused_kernel, n, groups, cols),
-        out_shape=jax.ShapeDtypeStruct((n * STRETCH, HQ * HD), jnp.bfloat16),
+        out_shape=pltpu.VMEM((n * STRETCH, HQ * HD), jnp.bfloat16),
         in_specs=[anywhere, anywhere, vmem, anywhere, smem, smem, vmem],
-        out_specs=anywhere,
+        out_specs=vmem,
         scratch_shapes=[
             pltpu.VMEM((n, groups, STRETCH, width), jnp.bfloat16),
             pltpu.VMEM((2 * cols, width), jnp.bfloat16),
@@ -578,8 +589,7 @@
             dma((n,)),
             dma((n, 2)),
             pltpu.VMEM((1, qkv_bias.shape[0]), jnp.float32),
-            pltpu.VMEM((n, STRETCH, HQ * HD), jnp.bfloat16),
-            dma((n,)),
+            pltpu.SemaphoreType.REGULAR,
         ],
         compiler_params=pltpu.CompilerParams(
             collective_id=0, has_side_effects=True, vmem_limit_bytes=56 * 2**20

time: 70.5 us -> 69.1 us (0.980)
  local copies, waits for them, and re-layouts: 1.87 us -> 0.8 us
    unnamed x1, local copies, waits for them, and re-layouts: 1.87 us -> 0.8 us
where the time goes in v5:
time: 69.1 us; the launch traced here: 68.9 us
  Pallas kernels  68.1 us (99%)
  local copies, waits for them, and re-layouts  0.8 us (1%)
    pallas_call x1, Pallas kernels, fused(): pl.pallas_call(functools.partial(fused_kernel, n, groups, cols), out_shap...  68.1 us

profile of v5, /device:TPU:0, one launch (start us, length us, event | category | flops | bytes accessed | tf_op | source)
XLA Modules:
  0.0 68.9 jit_solution(4068519135547923848)
XLA Ops:
  0.0 68.1 %shard_map.73 = bf16[64,4096]{1,0:T(8,128)(2,1)S(1)} custom-call(bf16[64,4096]{1,0:T(8,128)(2,1)} %tokens_ref.1, bf16[320,4096]{1,0:T(8,128)(2,1)} %bitcast.1, bf16[5120]{0:T(1024)(128)(2,1)} %bias_ref.1, bf16[4,1024,1024]{2,1,0:T(8,128)(2,1)} %cache_ref.1, s32[64]{0:T(128)} %lengths_ref.1, s32[64]{0:T(128)} %streams_ref.1, f32[1,128]{1,0:T(1,128)} %constant.2.clone.freq_ref), custom_call_target="tpu_custom_call" | custom-call | flops 3758096384 | bytes 13631488 | tf_op jit(solution)/shard_map/pallas_call | solution.py:569
  68.1 0.8 %copy.9 = bf16[64,4096]{1,0:T(8,128)(2,1)} copy(bf16[64,4096]{1,0:T(8,128)(2,1)S(1)} %shard_map.73) | data formatting | bytes 1048576

commit v6 on v5

--- a/solution.py
+++ b/solution.py
@@ -160,6 +160,7 @@
 
 MESH = pl.DeviceIdType.MESH
 LOG2E = 1.4426950408889634
+AHEAD = 2
 
 
 def fused_kernel(
@@ -192,6 +193,7 @@
     relay_sems,
     bias_all,
     partner_in,
+    partial,
 ):
     tp = lax.axis_index("tp")
     me = lax.axis_index("grp")
@@ -207,7 +209,10 @@
 
     def local_tokens(c):
         return pltpu.make_async_copy(
-            tokens_ref.at[pl.ds(pl.multiple_of(c * STRETCH, STRETCH), STRETCH)],
+            tokens_ref.at[
+                pl.ds(pl.multiple_of(c // 2 * STRETCH, STRETCH), STRETCH),
+                pl.ds(pl.multiple_of(c % 2 * width, HD), width),
+            ],
             tok.at[c, me],
             tok_local.at[c],
         )
@@ -272,29 +277,31 @@
         (main * (1 - side), HD // 2, main + HD // 2 * ((tp + side) % 2)),
     )
 
-    def weight_own(p):
+    def weight_own(q):
+        p, h = divmod(q, 2)
         start, size, at = pieces[p]
         return pltpu.make_async_copy(
-            weight_ref.at[pl.ds(pl.multiple_of(start, HD // 2), size)],
-            weights.at[pl.ds(pl.multiple_of(at, HD // 2), size)],
-            weight_sems.at[p, 0],
-        )
-
-    def weight_swap(p):
+            weight_ref.at[pl.ds(pl.multiple_of(start, HD // 2), size), pl.ds(h * width, width)],
+            weights.at[h, pl.ds(pl.multiple_of(at, HD // 2), size)],
+            weight_sems.at[q, 0],
+        )
+
+    def weight_swap(q):
+        p, h = divmod(q, 2)
         start, size, at = pieces[p]
         return pltpu.make_async_remote_copy(
-            src_ref=weight_ref.at[pl.ds(pl.multiple_of(start, HD // 2), size)],
-            dst_ref=weights.at[pl.ds(pl.multiple_of(at, HD // 2), size)],
-            send_sem=weight_sems.at[p, 1],
-            recv_sem=weight_sems.at[p, 2],
+            src_ref=weight_ref.at[pl.ds(pl.multiple_of(start, HD // 2), size), pl.ds(h * width, width)],
+            dst_ref=weights.at[h, pl.ds(pl.multiple_of(at, HD // 2), size)],
+            send_sem=weight_sems.at[q, 1],
+            recv_sem=weight_sems.at[q, 2],
             device_id={"tp": 1 - tp},
             device_id_type=MESH,
         )
 
-    for c in range(n):
+    for c in range(2 * n):
         local_tokens(c).start()
 
-    for p in range(2):
+    for p in range(4):
         weight_own(p).start()
     for c in range(n):
         cache_copy(c).start()
@@ -384,8 +391,6 @@
                 tok_copy(c, block, 1, me - 2).wait_send()
 
         relay_copy(c, depth).wait_send()
-        for d in range(1, groups):
-            part_copy(c, lax.rem(me + d, groups)).wait_send()
 
     def project(c):
         for level in range(chain):
@@ -400,13 +405,21 @@
                 rest_copy(c, block).wait_recv()
                 relay_copy(c, level).wait_recv()
 
-        rows = tok[c].reshape(groups * STRETCH, tok.shape[3])
-        product = lax.dot_general(rows, weights[...], nt, preferred_element_type=jnp.float32)
-        product = (product + bias[...]).astype(jnp.bfloat16)
-        outgoing[c] = product.reshape(groups, STRETCH, 2 * cols)
-        for d in range(1, groups):
-            part_copy(c, lax.rem(me + d, groups)).start()
-        incoming[c, me] = outgoing[c, me]
+        rows = tok[c].reshape(groups * STRETCH, width)
+        product = lax.dot_general(rows, weights[c % 2], nt, preferred_element_type=jnp.float32)
+
+        @pl.when(c % 2 == 0)
+        def _():
+            partial[...] = product + bias[...]
+
+        @pl.when(c % 2 == 1)
+        def _():
+            slot = c // 2
+            full = (partial[...] + product).astype(jnp.bfloat16)
+            outgoing[slot] = full.reshape(groups, STRETCH, 2 * cols)
+            for d in range(1, groups):
+                part_copy(slot, lax.rem(me + d, groups)).start()
+            incoming[slot, me] = outgoing[slot, me]
 
     lane = lax.broadcasted_iota(jnp.int32, (STRETCH, HD), 1)
     rows_all = STRETCH * GROUP
@@ -414,10 +427,12 @@
     half = groups // 2 * pair_heads
     middle = pair_heads // 2
 
-    def attention(c):
+    def arrive(c):
         for d in range(1, groups):
             part_arrival(c, lax.rem(me + d, groups)).wait_recv()
         cache_copy(c).wait()
+
+    def attention(c, key_heads):
         length = lengths_ref[streams_ref[first_slot + c]]
         cosine = cos_table[c]
         sine = sin_table[c]
@@ -447,7 +462,7 @@
             u = head(i).astype(jnp.float32)
             return (u * cosine + pltpu.roll(u, HD // 2, 1) * sine).astype(jnp.bfloat16)
 
-        for k in range(KVH):
+        for k in key_heads:
             queries = jnp.concatenate([rotated(k * GROUP + g) for g in range(GROUP)], axis=0)
             new_keys = rotated(HQ + k)
             new_values = head(HQ + KVH + k)
@@ -477,11 +492,12 @@
                     pl.ds(pl.multiple_of(c * STRETCH, STRETCH), STRETCH), h * HD : (h + 1) * HD
                 ] = result[g * STRETCH : (g + 1) * STRETCH]
 
-    send_own(0)
+    for c in range(AHEAD):
+        send_own(c)
 
     @pl.when(tp == 1)
     def _():
-        for p in range(2):
+        for p in range(4):
             weight_swap(p).start()
 
     for start in range(0, bias_ref.shape[0], 2 * HD):
@@ -509,49 +525,54 @@
         cos_table[c] = jnp.cos(angles)
         sin_table[c] = jnp.sin(angles) * sign
 
-    @pl.loop(0, n + 3)
+    def stage(i, low, body):
+        pl.when((i >= low) & (i < 2 * n + low))(lambda: body(i - low))
+
+    @pl.loop(0, 2 * n + chain + 1)
     def _(i):
-        @pl.when(i < n)
-        def _():
-            forward(i, 1)
-
-        @pl.when(i + 1 < n)
-        def _():
-            send_own(i + 1)
+        for s in range(1, chain):
+            stage(i, s - 1, functools.partial(forward, s=s))
+        stage(i, 1, relay)
+
+        @pl.when(i + AHEAD < 2 * n)
+        def _():
+            send_own(i + AHEAD)
 
         @pl.when((i == 0) & (tp == 0))
         def _():
             pl.semaphore_wait(partner_in, 1)
-            for p in range(2):
+            for p in range(4):
                 weight_swap(p).start()
 
-        @pl.when(((i >= 2) & (i < n)) | ((i > n) & (i >= 3)))
-        def _():
-            attention(jnp.where(i < n, i - 2, i - 3))
-
-        @pl.when(i < n)
-        def _():
-            relay(i)
-            for s in range(2, chain - 1):
-                forward(i, s)
-
-        @pl.when(i == 1)
-        def _():
-            for p in range(2):
+        @pl.when(i == chain - 1)
+        def _():
+            for p in range(4):
                 weight_own(p).wait()
                 weight_swap(p).wait()
 
-        @pl.when((i >= 1) & (i < n + 1))
-        def _():
-            project(i - 1)
-
-        @pl.when(i < n)
-        def _():
-            forward(i, chain - 1)
+        stage(i, chain - 1, project)
+
+        def first_heads(c):
+            @pl.when(c % 2 == 0)
+            def _():
+                arrive(c // 2)
+                attention(c // 2, range(KVH // 2))
+
+        def other_heads(c):
+            @pl.when(c % 2 == 1)
+            def _():
+                attention(c // 2, range(KVH // 2, KVH))
+
+        stage(i, chain + 1, lambda c: (first_heads(c), other_heads(c)) and None)
+
+    @pl.loop(0, 2 * n)
+    def _(c):
+        finish_sends(c)
 
     @pl.loop(0, n)
     def _(c):
-        finish_sends(c)
+        for d in range(1, groups):
+            part_copy(c, lax.rem(me + d, groups)).wait_send()
 
 
 def fused(tokens, qkv_weight, qkv_bias, cache, lengths, slot_stream):
@@ -572,24 +593,25 @@
         in_specs=[anywhere, anywhere, vmem, anywhere, smem, smem, vmem],
         out_specs=vmem,
         scratch_shapes=[
-            pltpu.VMEM((n, groups, STRETCH, width), jnp.bfloat16),
-            pltpu.VMEM((2 * cols, width), jnp.bfloat16),
+            pltpu.VMEM((2 * n, groups, STRETCH, width // 2), jnp.bfloat16),
+            pltpu.VMEM((2, 2 * cols, width // 2), jnp.bfloat16),
             pltpu.VMEM(cache.shape, jnp.bfloat16),
             pltpu.VMEM((1, 2 * cols), jnp.float32),
             pltpu.VMEM((n, groups, STRETCH, 2 * cols), jnp.bfloat16),
             pltpu.VMEM((n, groups, STRETCH, 2 * cols), jnp.bfloat16),
             pltpu.VMEM((n, STRETCH, HD), jnp.float32),
             pltpu.VMEM((n, STRETCH, HD), jnp.float32),
-            dma((n,)),
-            dma((n, groups, 3)),
+            dma((2 * n,)),
+            dma((2 * n, groups, 3)),
+            dma((2 * n, groups)),
             dma((n, groups)),
             dma((n, groups)),
-            dma((n, groups)),
-            dma((2, 3)),
+            dma((4, 3)),
             dma((n,)),
-            dma((n, 2)),
+            dma((2 * n, 2)),
             pltpu.VMEM((1, qkv_bias.shape[0]), jnp.float32),
             pltpu.SemaphoreType.REGULAR,
+            pltpu.VMEM((rows, 2 * cols), jnp.float32),
         ],
         compiler_params=pltpu.CompilerParams(
             collective_id=0, has_side_effects=True, vmem_limit_bytes=56 * 2**20

time: 69.1 us -> 72.7 us (1.052)
  Pallas kernels: 68.1 us -> 71.7 us
    pallas_call x1, Pallas kernels: 68.1 us -> 71.7 us  [fused(): pl.pallas_call(functools.partial(fused_kernel, n, groups, cols), out_shap...]
where the time goes in v6:
time: 72.7 us; the launch traced here: 72.5 us
  Pallas kernels  71.7 us (99%)
  local copies, waits for them, and re-layouts  0.8 us (1%)
    pallas_call x1, Pallas kernels, fused(): pl.pallas_call(functools.partial(fused_kernel, n, groups, cols), out_shap...  71.7 us

profile of v6, /device:TPU:0, one launch (start us, length us, event | category | flops | bytes accessed | tf_op | source)
XLA Modules:
  0.0 72.5 jit_solution(17000210379496921115)
XLA Ops:
  0.0 71.7 %shard_map.73 = bf16[64,4096]{1,0:T(8,128)(2,1)S(1)} custom-call(bf16[64,4096]{1,0:T(8,128)(2,1)} %tokens_ref.1, bf16[320,4096]{1,0:T(8,128)(2,1)} %bitcast.1, bf16[5120]{0:T(1024)(128)(2,1)} %bias_ref.1, bf16[4,1024,1024]{2,1,0:T(8,128)(2,1)} %cache_ref.1, s32[64]{0:T(128)} %lengths_ref.1, s32[64]{0:T(128)} %streams_ref.1, f32[1,128]{1,0:T(1,128)} %constant.2.clone.freq_ref), custom_call_target="tpu_custom_call" | custom-call | flops 3758096384 | bytes 13631488 | tf_op jit(solution)/shard_map/pallas_call | solution.py:590
  71.7 0.8 %copy.9 = bf16[64,4096]{1,0:T(8,128)(2,1)} copy(bf16[64,4096]{1,0:T(8,128)(2,1)S(1)} %shard_map.73) | data formatting | bytes 1048576

commit v7 on v5

--- a/solution.py
+++ b/solution.py
@@ -200,6 +200,8 @@
     side = me % 2
     across = depth * 2 + 1 - side
     paired = depth + 1 - 2 * (depth % 2)
+    at_end = (depth == 0) | (depth == chain - 1)
+    paired_at_end = (paired == 0) | (paired == chain - 1)
     width = tok.shape[3]
     split = width * 11 // 32 // HD * HD
     main = cols - HD // 2
@@ -236,8 +238,8 @@
             device_id_type=MESH,
         )
 
-    def relay_copy(c, level):
-        part = tok.at[c, level * 2 + 1 - side, :, pl.ds(0, split)]
+    def relay_copy(c, level, size):
+        part = tok.at[c, level * 2 + 1 - side, :, pl.ds(0, size)]
         return pltpu.make_async_remote_copy(
             src_ref=part,
             dst_ref=part,
@@ -328,7 +330,7 @@
             tok_copy(c, me, 1, me - 2).start()
 
     def send_across(c, block, shared):
-        @pl.when(shared)
+        @pl.when(shared & jnp.logical_not(paired_at_end))
         def _():
             rest_copy(c, block).start()
 
@@ -338,7 +340,14 @@
 
     def relay(c):
         tok_copy(c, across, 2, across).wait_recv()
-        relay_copy(c, depth).start()
+
+        @pl.when(at_end)
+        def _():
+            relay_copy(c, depth, width).start()
+
+        @pl.when(jnp.logical_not(at_end))
+        def _():
+            relay_copy(c, depth, split).start()
 
     def forward(c, s):
         @pl.when(depth >= s)
@@ -367,7 +376,7 @@
         for level in range(chain):
             block = level * 2 + side
 
-            @pl.when(level == paired)
+            @pl.when((level == paired) & jnp.logical_not(paired_at_end))
             def _():
                 rest_copy(c, block).wait_send()
 
@@ -383,7 +392,14 @@
             def _():
                 tok_copy(c, block, 1, me - 2).wait_send()
 
-        relay_copy(c, depth).wait_send()
+        @pl.when(at_end)
+        def _():
+            relay_copy(c, depth, width).wait_send()
+
+        @pl.when(jnp.logical_not(at_end))
+        def _():
+            relay_copy(c, depth, split).wait_send()
+
         for d in range(1, groups):
             part_copy(c, lax.rem(me + d, groups)).wait_send()
 
@@ -395,10 +411,14 @@
             def _():
                 tok_copy(c, block, 2, across).wait_recv()
 
-            @pl.when(level == paired)
+            @pl.when((level == paired) & paired_at_end)
+            def _():
+                relay_copy(c, level, width).wait_recv()
+
+            @pl.when((level == paired) & jnp.logical_not(paired_at_end))
             def _():
                 rest_copy(c, block).wait_recv()
-                relay_copy(c, level).wait_recv()
+                relay_copy(c, level, split).wait_recv()
 
         rows = tok[c].reshape(groups * STRETCH, tok.shape[3])
         product = lax.dot_general(rows, weights[...], nt, preferred_element_type=jnp.float32)

time: 69.1 us -> 68.8 us (level)
  no operation moved by 1% of the time
where the time goes in v7:
time: 68.8 us; the launch traced here: 68.6 us
  Pallas kernels  67.8 us (99%)
  local copies, waits for them, and re-layouts  0.8 us (1%)
    pallas_call x1, Pallas kernels, fused(): pl.pallas_call(functools.partial(fused_kernel, n, groups, cols), out_shap...  67.8 us

profile of v7, /device:TPU:0, one launch (start us, length us, event | category | flops | bytes accessed | tf_op | source)
XLA Modules:
  0.0 68.6 jit_solution(16576750280310576831)
XLA Ops:
  0.0 67.8 %shard_map.73 = bf16[64,4096]{1,0:T(8,128)(2,1)S(1)} custom-call(bf16[64,4096]{1,0:T(8,128)(2,1)} %tokens_ref.1, bf16[320,4096]{1,0:T(8,128)(2,1)} %bitcast.1, bf16[5120]{0:T(1024)(128)(2,1)} %bias_ref.1, bf16[4,1024,1024]{2,1,0:T(8,128)(2,1)} %cache_ref.1, s32[64]{0:T(128)} %lengths_ref.1, s32[64]{0:T(128)} %streams_ref.1, f32[1,128]{1,0:T(1,128)} %constant.2.clone.freq_ref), custom_call_target="tpu_custom_call" | custom-call | flops 3758096384 | bytes 13631488 | tf_op jit(solution)/shard_map/pallas_call | solution.py:589
  67.8 0.8 %copy.9 = bf16[64,4096]{1,0:T(8,128)(2,1)} copy(bf16[64,4096]{1,0:T(8,128)(2,1)S(1)} %shard_map.73) | data formatting | bytes 1048576

commit v8 on v7

--- a/solution.py
+++ b/solution.py
@@ -434,10 +434,12 @@
     half = groups // 2 * pair_heads
     middle = pair_heads // 2
 
-    def attention(c):
+    def arrive(c):
         for d in range(1, groups):
             part_arrival(c, lax.rem(me + d, groups)).wait_recv()
         cache_copy(c).wait()
+
+    def attention(c, key_heads):
         length = lengths_ref[streams_ref[first_slot + c]]
         cosine = cos_table[c]
         sine = sin_table[c]
@@ -467,7 +469,7 @@
             u = head(i).astype(jnp.float32)
             return (u * cosine + pltpu.roll(u, HD // 2, 1) * sine).astype(jnp.bfloat16)
 
-        for k in range(KVH):
+        for k in key_heads:
             queries = jnp.concatenate([rotated(k * GROUP + g) for g in range(GROUP)], axis=0)
             new_keys = rotated(HQ + k)
             new_values = head(HQ + KVH + k)
@@ -529,7 +531,7 @@
         cos_table[c] = jnp.cos(angles)
         sin_table[c] = jnp.sin(angles) * sign
 
-    @pl.loop(0, n + 3)
+    @pl.loop(0, n + 2)
     def _(i):
         @pl.when(i < n)
         def _():
@@ -545,9 +547,10 @@
             for p in range(2):
                 weight_swap(p).start()
 
-        @pl.when(((i >= 2) & (i < n)) | ((i > n) & (i >= 3)))
-        def _():
-            attention(jnp.where(i < n, i - 2, i - 3))
+        @pl.when(i >= 2)
+        def _():
+            arrive(i - 2)
+            attention(i - 2, range(KVH // 2))
 
         @pl.when(i < n)
         def _():
@@ -568,6 +571,10 @@
         @pl.when(i < n)
         def _():
             forward(i, chain - 1)
+
+        @pl.when(i >= 2)
+        def _():
+            attention(i - 2, range(KVH // 2, KVH))
 
     @pl.loop(0, n)
     def _(c):

time: 68.8 us -> 71 us (1.032)
  Pallas kernels: 67.8 us -> 70 us
    pallas_call x1, Pallas kernels: 67.8 us -> 70 us  [fused(): pl.pallas_call(functools.partial(fused_kernel, n, groups, cols), out_shap...]
where the time goes in v8:
time: 71 us; the launch traced here: 70.8 us
  Pallas kernels  70 us (99%)
  local copies, waits for them, and re-layouts  0.8 us (1%)
    pallas_call x1, Pallas kernels, fused(): pl.pallas_call(functools.partial(fused_kernel, n, groups, cols), out_shap...  70 us

profile of v8, /device:TPU:0, one launch (start us, length us, event | category | flops | bytes accessed | tf_op | source)
XLA Modules:
  0.0 70.8 jit_solution(1790780723882925692)
XLA Ops:
  0.0 70.0 %shard_map.73 = bf16[64,4096]{1,0:T(8,128)(2,1)S(1)} custom-call(bf16[64,4096]{1,0:T(8,128)(2,1)} %tokens_ref.1, bf16[320,4096]{1,0:T(8,128)(2,1)} %bitcast.1, bf16[5120]{0:T(1024)(128)(2,1)} %bias_ref.1, bf16[4,1024,1024]{2,1,0:T(8,128)(2,1)} %cache_ref.1, s32[64]{0:T(128)} %lengths_ref.1, s32[64]{0:T(128)} %streams_ref.1, f32[1,128]{1,0:T(1,128)} %constant.2.clone.freq_ref), custom_call_target="tpu_custom_call" | custom-call | flops 3758096384 | bytes 13631488 | tf_op jit(solution)/shard_map/pallas_call | solution.py:596
  70.0 0.8 %copy.9 = bf16[64,4096]{1,0:T(8,128)(2,1)} copy(bf16[64,4096]{1,0:T(8,128)(2,1)S(1)} %shard_map.73) | data formatting | bytes 1048576

commit v9 on v7

--- a/solution.py
+++ b/solution.py
@@ -497,7 +497,14 @@
                     pl.ds(pl.multiple_of(c * STRETCH, STRETCH), STRETCH), h * HD : (h + 1) * HD
                 ] = result[g * STRETCH : (g + 1) * STRETCH]
 
+    ahead = 2 - tp
     send_own(0)
+    if n > 1:
+
+        @pl.when(tp == 0)
+        def _():
+            send_own(1)
+
 
     @pl.when(tp == 1)
     def _():
@@ -535,9 +542,9 @@
         def _():
             forward(i, 1)
 
-        @pl.when(i + 1 < n)
-        def _():
-            send_own(i + 1)
+        @pl.when(i + ahead < n)
+        def _():
+            send_own(i + ahead)
 
         @pl.when((i == 0) & (tp == 0))
         def _():

time: 68.8 us -> 68.3 us (level)
  no operation moved by 1% of the time
where the time goes in v9:
time: 68.3 us; the launch traced here: 68.1 us
  Pallas kernels  67.3 us (99%)
  local copies, waits for them, and re-layouts  0.8 us (1%)
    pallas_call x1, Pallas kernels, fused(): pl.pallas_call(functools.partial(fused_kernel, n, groups, cols), out_shap...  67.3 us

profile of v9, /device:TPU:0, one launch (start us, length us, event | category | flops | bytes accessed | tf_op | source)
XLA Modules:
  0.0 68.1 jit_solution(5011123841769032161)
XLA Ops:
  0.0 67.3 %shard_map.73 = bf16[64,4096]{1,0:T(8,128)(2,1)S(1)} custom-call(bf16[64,4096]{1,0:T(8,128)(2,1)} %tokens_ref.1, bf16[320,4096]{1,0:T(8,128)(2,1)} %bitcast.1, bf16[5120]{0:T(1024)(128)(2,1)} %bias_ref.1, bf16[4,1024,1024]{2,1,0:T(8,128)(2,1)} %cache_ref.1, s32[64]{0:T(128)} %lengths_ref.1, s32[64]{0:T(128)} %streams_ref.1, f32[1,128]{1,0:T(1,128)} %constant.2.clone.freq_ref), custom_call_target="tpu_custom_call" | custom-call | flops 3758096384 | bytes 13631488 | tf_op jit(solution)/shard_map/pallas_call | solution.py:596
  67.3 0.8 %copy.9 = bf16[64,4096]{1,0:T(8,128)(2,1)} copy(bf16[64,4096]{1,0:T(8,128)(2,1)S(1)} %shard_map.73) | data formatting | bytes 1048576
